TPU v7x, 256 devices: a whole 4x4x8 slice. The times are simulated.
256 devices in a mesh: row: 16 (over x, z_hi), col: 16 (over y, z_lo, core).
Axes of the slice: x: 4, y: 4, z: 8 (z_hi: 4, z_lo: 2; z = z_hi * 2 + z_lo), core: 2. Of those that a mesh axis runs over, the one named last changes fastest.
Arguments:
- screened: float32 [12288, 12288], P('row', 'col'), may hold values from -0.0546875 to 0.0546875
- fit_coeffs: float32 [16, 12288, 256], P(None, 'row', 'col'), may hold values from -0.0546875 to 0.0546875
- coulomb_factors: float32 [16, 12288, 256], P(None, 'col', 'row'), may hold values from -6 to 6
- orbital_weights: float32 [16], replicated, may hold values from 0.2 to 2
Outputs:
- sigma: float32 [256, 256], P('row', 'col')
All inputs are finite; a program needn't handle non-finite values.
Results may differ from a plain program's by a relative error of at most 0.00024.
Values sent between devices are 32-bit elements; how exact they have to be, the bound alone decides.
A program may use at most 128 MiB of HBM per device.

v0:
```python
import jax
import jax.numpy as jnp
from jax import lax
from jax.sharding import PartitionSpec as P


def body(screened, fit_coeffs, coulomb_factors, orbital_weights):
    applied = jnp.einsum(
        "pq,mqk->mpk",
        screened,
        lax.all_gather(coulomb_factors, "row", axis=2, tiled=True),
        precision=lax.Precision.HIGHEST,
        preferred_element_type=jnp.float32,
    )
    scales = orbital_weights[:, None, None]
    summed = lax.psum_scatter(applied, "col", scatter_dimension=2, tiled=True)
    partial_rows = jnp.einsum(
        "mpn,mpk->nk",
        lax.all_gather(fit_coeffs, "col", axis=2, tiled=True) * scales,
        summed,
        precision=lax.Precision.HIGHEST,
        preferred_element_type=jnp.float32,
    )
    return lax.psum_scatter(partial_rows, "row", scatter_dimension=0, tiled=True)


def solution(mesh):
    placed = (P("row", "col"), P(None, "row", "col"), P(None, "col", "row"), P())
    return jax.shard_map(
        body, mesh=mesh, in_specs=placed, out_specs=P("row", "col"), check_vma=False
    )
```

profile of v0, /device:TPU:1, one launch (start us, length us, event | category | flops | bytes accessed | tf_op | source)
XLA Modules:
  0.0 495.3 jit_solution(17844808818891329470)
XLA Ops:
  6.5 0.0 copy-start
  6.5 0.0 all-gather.5.cloned.1.call-start
  6.5 0.7 all-gather.5.cloned.1.call-update
  7.3 0.0 all-gather.3.cloned.1.call-start
  7.3 0.7 all-gather.3.cloned.1.call-update
  8.0 0.0 reduce-scatter.3.cloned.1.call-start
  8.1 161.9 %all-gather.5.cloned.1.call-done = f32[16,768,256]{1,2,0:T(8,128)} async-done(((f32[16,768,16]{1,2,0:T(8,128)}), f32[16,768,256]{1,2,0:T(8,128)}) %all-gather.5.cloned.1.call-update) | async-done | bytes 12582928 | tf_op jit(solution)/shard_map/all_gather | solution.py:11
  169.9 0.0 copy-done
  169.9 34.5 %convolution_bitcast_fusion = f32[16,768,256]{1,2,0:T(8,128)} fusion(f32[16,768,256]{1,2,0:T(8,128)} %all-gather.5.cloned.1.call-done, f32[768,768]{1,0:T(8,128)S(1)} %copy-done), kind=kOutput, calls=%fused_computation.3 | convolution fusion | flops 28991029248 | bytes 27525120 | tf_op jit(solution)/shard_map/pq,mqk->mpk/dot_general | solution.py:8
  204.5 0.0 copy-start.1
  204.5 0.0 reduce-scatter.3.cloned.1.call-update
  204.5 0.2 reduce-scatter.5.cloned.1.call-start
  204.7 43.2 %all-gather.3.cloned.1.call-done = f32[16,768,256]{1,2,0:T(8,128)} async-done(((f32[16,768,16]{1,2,0:T(8,128)}), f32[16,768,256]{1,2,0:T(8,128)}) %all-gather.3.cloned.1.call-update) | async-done | bytes 12582928 | tf_op jit(solution)/shard_map/all_gather | solution.py:19
  247.9 144.0 %reduce-scatter.3.cloned.1.call-done = f32[16,768,16]{1,2,0:T(8,128)} async-done(((f32[16,768,256]{1,2,0:T(8,128)}), f32[16,768,16]{1,2,0:T(8,128)}) %reduce-scatter.3.cloned.1.call-update) | async-done | bytes 786448 | tf_op jit(solution)/shard_map/reduce_scatter | solution.py:16
  391.9 0.0 copy-done.1
  391.9 13.3 %fusion.4 = f32[256,16]{1,0:T(8,128)} fusion(f32[16,768,16]{1,2,0:T(8,128)} %reduce-scatter.3.cloned.1.call-done, f32[16,768,256]{1,2,0:T(8,128)} %all-gather.3.cloned.1.call-done, f32[16]{0:T(128)S(1)} %copy-done.1), kind=kOutput, calls=%fused_computation.5 | convolution fusion | flops 607125504 | bytes 13385792 | tf_op jit(solution)/shard_map/mpn,mpk->nk/dot_general | solution.py:17
  405.2 0.0 reduce-scatter.5.cloned.1.call-update
  405.2 83.5 %reduce-scatter.5.cloned.1.call-done = f32[16,16]{1,0:T(8,128)} async-done(((f32[256,16]{1,0:T(8,128)}), f32[16,16]{1,0:T(8,128)}) %reduce-scatter.5.cloned.1.call-update) | async-done | bytes 1040 | tf_op jit(solution)/shard_map/reduce_scatter | solution.py:24
Async XLA Ops:
  6.5 163.4 %copy-start = (f32[768,768]{1,0:T(8,128)S(1)}, f32[768,768]{1,0:T(8,128)}, u32[]{:S(2)}) copy-start(f32[768,768]{1,0:T(8,128)} %param.4) | copy-start | bytes 7077892
  6.5 163.4 %all-gather.5.cloned.1.call-start = ((), (), s32[]{:S(2)}) async-start(), calls=%async_computation.3 | async-start | bytes 13369344 | tf_op jit(solution)/shard_map/all_gather | solution.py:11
  7.3 240.6 %all-gather.3.cloned.1.call-start = ((), (), s32[]{:S(2)}) async-start(), calls=%async_computation.2 | async-start | bytes 13369344 | tf_op jit(solution)/shard_map/all_gather | solution.py:19
  8.0 383.9 %reduce-scatter.3.cloned.1.call-start = ((), (), s32[]{:S(2)}) async-start(), calls=%async_computation.4 | async-start | bytes 13369344 | tf_op jit(solution)/shard_map/reduce_scatter | solution.py:16
  204.5 187.4 %copy-start.1 = (f32[16]{0:T(128)S(1)}, f32[16]{0:T(128)}, u32[]{:S(2)}) copy-start(f32[16]{0:T(128)} %param.7) | copy-start | bytes 196
  204.5 284.2 %reduce-scatter.5.cloned.1.call-start = ((), (), s32[]{:S(2)}) async-start(), calls=%async_computation.5 | async-start | bytes 139264 | tf_op jit(solution)/shard_map/reduce_scatter | solution.py:24
Sparse Core Ops, SparseCore 0:
  9.8 160.1 all-gather.4
  171.7 76.1 all-gather.2
  250.5 141.4 reduce-scatter.2
  405.3 83.3 reduce-scatter.4
where the time goes:
time: 496 us; the launch traced here: 495 us
  waiting for transfers between devices  434 us (88%)
  matrix products  47.8 us (10%)
  between operations  13.1 us (3%)
    all_gather x1, waiting for transfers between devices, body(): lax.all_gather(coulomb_factors, 'row', axis=2, tiled=True)  162 us
    reduce_scatter x1, waiting for transfers between devices, body(): summed = lax.psum_scatter(applied, 'col', scatter_dimension=2, tiled=True)  144 us
    reduce_scatter x1, waiting for transfers between devices, body(): lax.psum_scatter(partial_rows, 'row', scatter_dimension=0, tiled=True)  83.5 us
    all_gather x1, waiting for transfers between devices, body(): lax.all_gather(fit_coeffs, 'col', axis=2, tiled=True) * scales  43.2 us
    dot_general x1, matrix products, body(): jnp.einsum('pq,mqk->mpk', screened, lax.all_gather(coulomb_factors, 'row'...  34.5 us
    dot_general x1, matrix products, body(): jnp.einsum('mpn,mpk->nk', lax.all_gather(fit_coeffs, 'col', axis=2, tiled...  13.3 us
  transfers between devices with their start and end apart: 4, of which 4 were waited for; matrix products, arithmetic and copies ran while one was open for 7% of the time, Pallas kernels for 0%

commit v1 on v0

v1 whole, which is shorter than its diff:
```python
import functools

import jax
import jax.numpy as jnp
from jax import lax
from jax.experimental import pallas as pl
from jax.experimental.pallas import tpu as pltpu
from jax.sharding import PartitionSpec as P

MESH = pl.DeviceIdType.MESH
AHEAD = 2
LAG = 3
NT = (((1,), (1,)), ((), ()))


def split(v):
    high = v.astype(jnp.bfloat16)
    return high, (v - high.astype(jnp.float32)).astype(jnp.bfloat16)


def kernel(
    w_ref, c_ref, b_ref, scale_ref, out_ref,
    cbuf, bbuf, wfull, whigh, wlow, sig, part1, half, part2, turned,
    load_sem, c_recv, b_recv, c_send, b_send, recv1, recv2, send1, send2,
):
    orbitals, states, aux = c_ref.shape
    row, col = lax.axis_index("row"), lax.axis_index("col")
    x, zh = row // 4, row % 4
    y, zl, core = col // 4, (col // 2) % 2, col % 2

    def row_of(x_at, zh_at):
        return (x_at + 4) % 4 * 4 + (zh_at + 4) % 4

    def col_of(y_at, zl_at, core_at):
        return (y_at + 4) % 4 * 4 + zl_at * 2 + core_at

    barrier = pltpu.get_barrier_semaphore()
    for step in range(1, 16):
        pl.semaphore_signal(barrier, inc=1, device_id=(row, (col + step) % 16), device_id_type=MESH)
        pl.semaphore_signal(barrier, inc=1, device_id=((row + step) % 16, col), device_id_type=MESH)

    loads = [
        pltpu.make_async_copy(w_ref, wfull, load_sem.at[0]),
        pltpu.make_async_copy(c_ref, cbuf.at[col], load_sem.at[1]),
        pltpu.make_async_copy(b_ref, bbuf.at[row], load_sem.at[2]),
    ]
    for load in loads:
        load.start()
    sig[...] = jnp.zeros_like(sig)
    pl.semaphore_wait(barrier, 30)

    def c_copy(g, piece, edge, to, own=False):
        return pltpu.make_async_remote_copy(
            src_ref=c_ref.at[g] if own else cbuf.at[piece, g],
            dst_ref=cbuf.at[piece, g],
            send_sem=c_send.at[edge],
            recv_sem=c_recv.at[piece, g],
            device_id=(row, to),
            device_id_type=MESH,
        )

    def b_copy(g, piece, edge, to, own=False):
        return pltpu.make_async_remote_copy(
            src_ref=b_ref.at[g] if own else bbuf.at[piece, g],
            dst_ref=bbuf.at[piece, g],
            send_sem=b_send.at[edge],
            recv_sem=b_recv.at[piece, g],
            device_id=(to, col),
            device_id_type=MESH,
        )

    def own_sends(g):
        b_copy(g, row, 0, row_of(x, zh + 1), True).start()
        b_copy(g, row, 1, row_of(x, zh - 1), True).start()
        b_copy(g, row, 2, row_of(x + 1, zh), True).start()
        b_copy(g, row, 3, row_of(x - 1, zh), True).start()
        c_copy(g, col, 0, col_of(y, 1 - zl, core), True).start()
        c_copy(g, col, 1, col_of(y + 1, zl, core), True).start()
        c_copy(g, col, 2, col_of(y - 1, zl, core), True).start()
        c_copy(g, col, 3, col_of(y, zl, 1 - core), True).start()

    def got_c(g, piece):
        c_copy(g, piece, 0, col).wait_recv()

    def got_b(g, piece):
        b_copy(g, piece, 0, row).wait_recv()

    def first_hop(g):
        way = 1 - 2 * (g % 2)
        for at, side in enumerate((way, -way)):
            piece = row_of(x, zh - side)
            got_b(g, piece)
            if at == 0:
                b_copy(g, piece, 4, row_of(x, zh + way)).start()
            b_copy(g, piece, 5 + 2 * at, row_of(x + 1, zh)).start()
            b_copy(g, piece, 6 + 2 * at, row_of(x - 1, zh)).start()
        piece = col_of(y, 1 - zl, core)
        got_c(g, piece)
        c_copy(g, piece, 4, col_of(y + 1, zl, core)).start()
        c_copy(g, piece, 5, col_of(y - 1, zl, core)).start()
        c_copy(g, piece, 6, col_of(y, zl, 1 - core)).start()

    def second_hop(g):
        way = 1 - 2 * (g % 2)
        piece = row_of(x, zh + 2)
        got_b(g, piece)
        b_copy(g, piece, 9, row_of(x + 1, zh)).start()
        b_copy(g, piece, 10, row_of(x - 1, zh)).start()
        for at, off in enumerate((0, 1, -1, 2)):
            piece = row_of(x - way, zh + off)
            got_b(g, piece)
            b_copy(g, piece, 11 + at, row_of(x + way, zh)).start()
        for at in range(2):
            piece = col_of(y - way, at, core)
            got_c(g, piece)
            c_copy(g, piece, 7 + at, col_of(y + way, zl, core)).start()
            c_copy(g, piece, 9 + at, col_of(y, zl, 1 - core)).start()
            piece = col_of(y + way, at, core)
            got_c(g, piece)
            c_copy(g, piece, 11 + at, col_of(y, zl, 1 - core)).start()

    def third_hop(g):
        for at in range(2):
            piece = col_of(y + 2, at, core)
            got_c(g, piece)
            c_copy(g, piece, 13 + at, col_of(y, zl, 1 - core)).start()

    def products(g):
        way = 1 - 2 * (g % 2)
        for y_at in range(4):
            for zl_at in range(2):
                got_c(g, col_of(y_at, zl_at, 1 - core))
        c_high, c_low = split(cbuf[:, g].reshape(16 * states, aux))
        t = jnp.dot(c_high, whigh[...], preferred_element_type=jnp.float32)
        t += jnp.dot(c_high, wlow[...], preferred_element_type=jnp.float32)
        t += jnp.dot(c_low, whigh[...], preferred_element_type=jnp.float32)
        t_high, t_low = split(t * scale_ref[g])
        for off in range(4):
            got_b(g, row_of(x + way, zh + off))
            got_b(g, row_of(x + 2, zh + off))
        b_high, b_low = split(bbuf[:, g].reshape(16 * states, aux))
        s = lax.dot_general(b_high, t_high, NT, preferred_element_type=jnp.float32)
        s += lax.dot_general(b_high, t_low, NT, preferred_element_type=jnp.float32)
        s += lax.dot_general(b_low, t_high, NT, preferred_element_type=jnp.float32)
        sig[...] += s

    for g in range(AHEAD):
        own_sends(g)
    for load in loads:
        load.wait()
    w_high, w_low = split(wfull[...])
    whigh[...] = w_high
    wlow[...] = w_low

    @pl.loop(0, orbitals + LAG)
    def tick(t):
        @pl.when(t + AHEAD < orbitals)
        def _():
            own_sends(t + AHEAD)

        @pl.when(t < orbitals)
        def _():
            first_hop(t)

        @pl.when((t >= 1) & (t < orbitals + 1))
        def _():
            second_hop(t - 1)

        @pl.when((t >= 2) & (t < orbitals + 2))
        def _():
            third_hop(t - 2)

        @pl.when(t >= LAG)
        def _():
            products(t - LAG)

    def copy1(step):
        to = (col + step) % 16
        return pltpu.make_async_remote_copy(
            src_ref=sig.at[pl.ds(pl.multiple_of(to * states, states), states)],
            dst_ref=part1.at[col],
            send_sem=send1.at[step],
            recv_sem=recv1.at[col],
            device_id=(row, to),
            device_id_type=MESH,
        )

    def copy2(step):
        to = (row + step) % 16
        return pltpu.make_async_remote_copy(
            src_ref=half.at[to // 8],
            dst_ref=part2.at[row],
            send_sem=send2.at[step],
            recv_sem=recv2.at[row],
            device_id=(to, col),
            device_id_type=MESH,
        )

    for step in range(1, 16):
        copy1(step).start()
    total = sig[pl.ds(pl.multiple_of(col * states, states), states), :]
    for step in range(1, 16):
        piece = (col + step) % 16
        pltpu.make_async_copy(part1.at[piece], part1.at[piece], recv1.at[piece]).wait()
        total += part1[piece]
    half[0] = total[:, :128]
    half[1] = total[:, 128:]
    for step in range(1, 16):
        copy2(step).start()
    total = half[row // 8]
    for step in range(1, 16):
        piece = (row + step) % 16
        pltpu.make_async_copy(part2.at[piece], part2.at[piece], recv2.at[piece]).wait()
        total += part2[piece]
    turned[...] = total.T
    out_ref[...] = turned[pl.ds(pl.multiple_of(row % 8 * states, states), states), :]

    for step in range(1, 16):
        copy1(step).wait_send()
        copy2(step).wait_send()
    for edge in range(15):
        pltpu.make_async_copy(c_ref, cbuf.at[0], c_send.at[edge]).wait()
        pltpu.make_async_copy(b_ref, bbuf.at[0], b_send.at[edge]).wait()


def body(screened, fit_coeffs, coulomb_factors, orbital_weights):
    orbitals, aux, states = fit_coeffs.shape
    f32, bf16 = jnp.float32, jnp.bfloat16
    dma = pltpu.SemaphoreType.DMA
    return pl.pallas_call(
        kernel,
        out_shape=jax.ShapeDtypeStruct((states, states), f32),
        in_specs=[pl.BlockSpec(memory_space=pl.ANY)] * 3 + [pl.BlockSpec(memory_space=pltpu.SMEM)],
        out_specs=pl.BlockSpec(memory_space=pltpu.VMEM),
        scratch_shapes=[
            pltpu.VMEM((16, orbitals, states, aux), f32),
            pltpu.VMEM((16, orbitals, states, aux), f32),
            pltpu.VMEM((aux, aux), f32),
            pltpu.VMEM((aux, aux), bf16),
            pltpu.VMEM((aux, aux), bf16),
            pltpu.VMEM((16 * states, 16 * states), f32),
            pltpu.VMEM((16, states, 16 * states), f32),
            pltpu.VMEM((2, states, 128), f32),
            pltpu.VMEM((16, states, 128), f32),
            pltpu.VMEM((128, states), f32),
            dma((3,)),
            dma((16, orbitals)),
            dma((16, orbitals)),
            dma((15,)),
            dma((15,)),
            dma((16,)),
            dma((16,)),
            dma((16,)),
            dma((16,)),
        ],
        compiler_params=pltpu.CompilerParams(
            collective_id=0, has_side_effects=True, vmem_limit_bytes=48 * 1024 * 1024
        ),
        cost_estimate=pl.CostEstimate(flops=20_000_000_000, bytes_accessed=4_000_000, transcendentals=0),
    )(
        screened,
        jnp.transpose(fit_coeffs, (0, 2, 1)),
        jnp.transpose(coulomb_factors, (0, 2, 1)),
        orbital_weights,
    )


def solution(mesh):
    placed = (P("row", "col"), P(None, "row", "col"), P(None, "col", "row"), P())
    return jax.shard_map(
        body, mesh=mesh, in_specs=placed, out_specs=P("row", "col"), check_vma=False
    )
```

time: 496 us -> 183 us (0.37)
  waiting for transfers between devices: 434 us -> 0 us
  Pallas kernels: 0 us -> 177 us
  matrix products: 47.8 us -> 0 us
  between operations: 13.1 us -> 0.01 us
  local copies, waits for them, and re-layouts: 0.01 us -> 5.19 us
    reduce_scatter x2 -> x0, waiting for transfers between devices: 228 us -> none  [the longest x1 144 us: body(): summed = lax.psum_scatter(applied, 'col', scatter_dimension=2, tiled=True)]
    all_gather x2 -> x0, waiting for transfers between devices: 205 us -> none  [the longest x1 162 us: body(): lax.all_gather(coulomb_factors, 'row', axis=2, tiled=True)]
    pallas_call x0 -> x1, Pallas kernels: none -> 177 us  [body(): pl.pallas_call(kernel, out_shape=jax.ShapeDtypeStruct((states, states), f...]
    dot_general x2 -> x0, matrix products: 47.8 us -> none  [the longest x1 34.5 us: body(): jnp.einsum('pq,mqk->mpk', screened, lax.all_gather(coulomb_factors, 'row'...]
    unnamed x4 -> x9, local copies, waits for them, and re-layouts: 0.01 us -> 5.19 us
  transfers between devices with their start and end apart: 4 -> 0, of which waited for: 4 -> 0; matrix products, arithmetic and copies ran while one was open for 7% -> 0% of each run, Pallas kernels for 0% -> 0%
where the time goes in v1:
time: 183 us
  Pallas kernels  177 us (97%)
  local copies, waits for them, and re-layouts  5.19 us (3%)
    pallas_call x1, Pallas kernels, body(): pl.pallas_call(kernel, out_shape=jax.ShapeDtypeStruct((states, states), f...  177 us
    unnamed x9, local copies, waits for them, and re-layouts  5.19 us

profile of v1, /device:TPU:1, one launch (start us, length us, event | category | flops | bytes accessed | tf_op | source)
XLA Modules:
  0.0 182.6 jit_solution(2804550687591063751)
XLA Ops:
  0.0 0.0 copy-start
  0.0 1.7 copy-done
  1.7 0.0 copy-start.1
  1.7 1.1 copy-done.1
  2.8 0.0 copy-start.2
  2.8 1.1 copy-done.2
  3.9 0.0 copy-start.3
  3.9 0.7 copy-done.3
  4.6 177.4 %shard_map.46 = f32[16,16]{1,0:T(8,128)S(1)} custom-call(f32[768,768]{1,0:T(8,128)S(1)} %copy-done, f32[16,16,768]{2,1,0:T(8,128)S(1)} %bitcast.2, f32[16,16,768]{2,1,0:T(8,128)S(1)} %bitcast.3, f32[16]{0:T(128)S(1)} %copy-done.3), custom_call_target="tpu_custom_call" | custom-call | flops 20000000000 | bytes 4000000 | tf_op jit(solution)/shard_map/pallas_call | solution.py:230
  182.0 0.6 copy.6
Async XLA Ops:
  0.0 1.7 copy-start
  1.7 1.1 copy-start.1
  2.8 1.1 copy-start.2
  3.9 0.7 copy-start.3

commit v2 on v1

--- a/solution.py
+++ b/solution.py
@@ -8,8 +8,11 @@
 from jax.sharding import PartitionSpec as P
 
 MESH = pl.DeviceIdType.MESH
-AHEAD = 2
-LAG = 3
+AHEAD = 3
+LAG = 4
+X_FIRST = (4, 11)
+B_RELAY, B_NEAR, B_FAR, B_SPREAD, B_LAST, B_KINDS = 0, 1, 2, 3, 6, 7
+C_PAIR, C_NEAR, C_FAR, C_CORE, C_KINDS = 0, 1, 3, 5, 6
 NT = (((1,), (1,)), ((), ()))
 
 
@@ -49,95 +52,116 @@
     sig[...] = jnp.zeros_like(sig)
     pl.semaphore_wait(barrier, 30)
 
-    def c_copy(g, piece, edge, to, own=False):
+    def c_copy(g, piece, edge, kind, to, own=False):
         return pltpu.make_async_remote_copy(
             src_ref=c_ref.at[g] if own else cbuf.at[piece, g],
             dst_ref=cbuf.at[piece, g],
             send_sem=c_send.at[edge],
-            recv_sem=c_recv.at[piece, g],
+            recv_sem=c_recv.at[kind, g],
             device_id=(row, to),
             device_id_type=MESH,
         )
 
-    def b_copy(g, piece, edge, to, own=False):
+    def b_copy(g, piece, edge, kind, to, own=False):
         return pltpu.make_async_remote_copy(
             src_ref=b_ref.at[g] if own else bbuf.at[piece, g],
             dst_ref=bbuf.at[piece, g],
             send_sem=b_send.at[edge],
-            recv_sem=b_recv.at[piece, g],
+            recv_sem=b_recv.at[kind, g],
             device_id=(to, col),
             device_id_type=MESH,
         )
 
+    def got_c(g, kind, pieces=1):
+        block = cbuf.at[pl.ds(0, pieces), g]
+        pltpu.make_async_copy(block, block, c_recv.at[kind, g]).wait()
+
+    def got_b(g, kind, pieces=1):
+        block = bbuf.at[pl.ds(0, pieces), g]
+        pltpu.make_async_copy(block, block, b_recv.at[kind, g]).wait()
+
+    def route(g):
+        x_first = jnp.where(functools.reduce(jnp.logical_or, [g == one for one in X_FIRST]), 1, 0)
+        way = 1 - 2 * (g % 2)
+
+        def at(first, second):
+            return row_of(
+                x + second + (first - second) * x_first, zh + first + (second - first) * x_first
+            )
+
+        return at, way
+
     def own_sends(g):
-        b_copy(g, row, 0, row_of(x, zh + 1), True).start()
-        b_copy(g, row, 1, row_of(x, zh - 1), True).start()
-        b_copy(g, row, 2, row_of(x + 1, zh), True).start()
-        b_copy(g, row, 3, row_of(x - 1, zh), True).start()
-        c_copy(g, col, 0, col_of(y, 1 - zl, core), True).start()
-        c_copy(g, col, 1, col_of(y + 1, zl, core), True).start()
-        c_copy(g, col, 2, col_of(y - 1, zl, core), True).start()
-        c_copy(g, col, 3, col_of(y, zl, 1 - core), True).start()
-
-    def got_c(g, piece):
-        c_copy(g, piece, 0, col).wait_recv()
-
-    def got_b(g, piece):
-        b_copy(g, piece, 0, row).wait_recv()
+        at, way = route(g)
+        b_copy(g, row, 0, B_RELAY, at(way, 0), True).start()
+        b_copy(g, row, 1, B_NEAR, at(-way, 0), True).start()
+        c_copy(g, col, 0, C_PAIR, col_of(y, 1 - zl, core), True).start()
+        b_copy(g, row, 2, B_SPREAD, at(0, way), True).start()
+        b_copy(g, row, 3, B_LAST, at(0, -way), True).start()
+        c_copy(g, col, 1, C_NEAR, col_of(y + 1, zl, core), True).start()
+        c_copy(g, col, 2, C_NEAR, col_of(y - 1, zl, core), True).start()
+        c_copy(g, col, 3, C_CORE, col_of(y, zl, 1 - core), True).start()
 
     def first_hop(g):
-        way = 1 - 2 * (g % 2)
-        for at, side in enumerate((way, -way)):
-            piece = row_of(x, zh - side)
-            got_b(g, piece)
-            if at == 0:
-                b_copy(g, piece, 4, row_of(x, zh + way)).start()
-            b_copy(g, piece, 5 + 2 * at, row_of(x + 1, zh)).start()
-            b_copy(g, piece, 6 + 2 * at, row_of(x - 1, zh)).start()
+        at, way = route(g)
+        got_b(g, B_RELAY)
+        piece = at(-way, 0)
+        b_copy(g, piece, 4, B_FAR, at(way, 0)).start()
+        b_copy(g, piece, 5, B_SPREAD + 1, at(0, way)).start()
+        b_copy(g, piece, 6, B_LAST, at(0, -way)).start()
+        got_b(g, B_NEAR)
+        piece = at(way, 0)
+        b_copy(g, piece, 7, B_SPREAD + 1, at(0, way)).start()
+        b_copy(g, piece, 8, B_LAST, at(0, -way)).start()
+        got_c(g, C_PAIR)
         piece = col_of(y, 1 - zl, core)
-        got_c(g, piece)
-        c_copy(g, piece, 4, col_of(y + 1, zl, core)).start()
-        c_copy(g, piece, 5, col_of(y - 1, zl, core)).start()
-        c_copy(g, piece, 6, col_of(y, zl, 1 - core)).start()
+        c_copy(g, piece, 4, C_NEAR + 1, col_of(y + 1, zl, core)).start()
+        c_copy(g, piece, 5, C_NEAR + 1, col_of(y - 1, zl, core)).start()
+        c_copy(g, piece, 6, C_CORE, col_of(y, zl, 1 - core)).start()
+        got_b(g, B_SPREAD)
+        b_copy(g, at(0, -way), 9, B_LAST, at(0, way)).start()
+        c_spread(g, 0, way)
+
+    def c_spread(g, far, way):
+        got_c(g, C_NEAR + far, 2)
+        zl_at = zl + far - 2 * zl * far
+        piece = col_of(y - way, zl_at, core)
+        c_copy(g, piece, 7 + far, C_FAR + far, col_of(y + way, zl, core)).start()
+        c_copy(g, piece, 9 + far, C_CORE, col_of(y, zl, 1 - core)).start()
+        piece = col_of(y + way, zl_at, core)
+        c_copy(g, piece, 11 + far, C_CORE, col_of(y, zl, 1 - core)).start()
+
+    def c_far(g, far):
+        got_c(g, C_FAR + far)
+        piece = col_of(y + 2, zl + far - 2 * zl * far, core)
+        c_copy(g, piece, 13 + far, C_CORE, col_of(y, zl, 1 - core)).start()
 
     def second_hop(g):
-        way = 1 - 2 * (g % 2)
-        piece = row_of(x, zh + 2)
-        got_b(g, piece)
-        b_copy(g, piece, 9, row_of(x + 1, zh)).start()
-        b_copy(g, piece, 10, row_of(x - 1, zh)).start()
-        for at, off in enumerate((0, 1, -1, 2)):
-            piece = row_of(x - way, zh + off)
-            got_b(g, piece)
-            b_copy(g, piece, 11 + at, row_of(x + way, zh)).start()
-        for at in range(2):
-            piece = col_of(y - way, at, core)
-            got_c(g, piece)
-            c_copy(g, piece, 7 + at, col_of(y + way, zl, core)).start()
-            c_copy(g, piece, 9 + at, col_of(y, zl, 1 - core)).start()
-            piece = col_of(y + way, at, core)
-            got_c(g, piece)
-            c_copy(g, piece, 11 + at, col_of(y, zl, 1 - core)).start()
+        at, way = route(g)
+        got_b(g, B_FAR)
+        piece = at(2, 0)
+        b_copy(g, piece, 10, B_SPREAD + 2, at(0, way)).start()
+        b_copy(g, piece, 11, B_LAST, at(0, -way)).start()
+        got_b(g, B_SPREAD + 1, 2)
+        b_copy(g, at(1, -way), 12, B_LAST, at(0, way)).start()
+        b_copy(g, at(-1, -way), 13, B_LAST, at(0, way)).start()
+        c_spread(g, 1, way)
+        c_far(g, 0)
 
     def third_hop(g):
-        for at in range(2):
-            piece = col_of(y + 2, at, core)
-            got_c(g, piece)
-            c_copy(g, piece, 13 + at, col_of(y, zl, 1 - core)).start()
+        at, way = route(g)
+        got_b(g, B_SPREAD + 2)
+        b_copy(g, at(2, -way), 14, B_LAST, at(0, way)).start()
+        c_far(g, 1)
 
     def products(g):
-        way = 1 - 2 * (g % 2)
-        for y_at in range(4):
-            for zl_at in range(2):
-                got_c(g, col_of(y_at, zl_at, 1 - core))
+        got_c(g, C_CORE, 8)
         c_high, c_low = split(cbuf[:, g].reshape(16 * states, aux))
         t = jnp.dot(c_high, whigh[...], preferred_element_type=jnp.float32)
         t += jnp.dot(c_high, wlow[...], preferred_element_type=jnp.float32)
         t += jnp.dot(c_low, whigh[...], preferred_element_type=jnp.float32)
         t_high, t_low = split(t * scale_ref[g])
-        for off in range(4):
-            got_b(g, row_of(x + way, zh + off))
-            got_b(g, row_of(x + 2, zh + off))
+        got_b(g, B_LAST, 8)
         b_high, b_low = split(bbuf[:, g].reshape(16 * states, aux))
         s = lax.dot_general(b_high, t_high, NT, preferred_element_type=jnp.float32)
         s += lax.dot_general(b_high, t_low, NT, preferred_element_type=jnp.float32)
@@ -244,8 +268,8 @@
             pltpu.VMEM((16, states, 128), f32),
             pltpu.VMEM((128, states), f32),
             dma((3,)),
-            dma((16, orbitals)),
-            dma((16, orbitals)),
+            dma((C_KINDS, orbitals)),
+            dma((B_KINDS, orbitals)),
             dma((15,)),
             dma((15,)),
             dma((16,)),
@@ -254,7 +278,7 @@
             dma((16,)),
         ],
         compiler_params=pltpu.CompilerParams(
-            collective_id=0, has_side_effects=True, vmem_limit_bytes=48 * 1024 * 1024
+            collective_id=0, has_side_effects=True, vmem_limit_bytes=63 * 1024 * 1024
         ),
         cost_estimate=pl.CostEstimate(flops=20_000_000_000, bytes_accessed=4_000_000, transcendentals=0),
     )(

time: 183 us -> 143 us (0.78)
  Pallas kernels: 177 us -> 142 us
  local copies, waits for them, and re-layouts: 5.19 us -> 1.3 us
    pallas_call x1, Pallas kernels: 177 us -> 142 us  [body(): pl.pallas_call(kernel, out_shape=jax.ShapeDtypeStruct((states, states), f...]
    unnamed x9 -> x1, local copies, waits for them, and re-layouts: 5.19 us -> 1.3 us
where the time goes in v2:
time: 143 us
  Pallas kernels  142 us (99%)
    pallas_call x1, Pallas kernels, body(): pl.pallas_call(kernel, out_shape=jax.ShapeDtypeStruct((states, states), f...  142 us

profile of v2, /device:TPU:1, one launch (start us, length us, event | category | flops | bytes accessed | tf_op | source)
XLA Modules:
  0.0 143.0 jit_solution(9216196734480382615)
XLA Ops:
  0.0 141.7 %shard_map.46 = f32[16,16]{1,0:T(8,128)} custom-call(f32[768,768]{1,0:T(8,128)} %w_ref.1, f32[16,16,768]{2,1,0:T(8,128)} %bitcast.2, f32[16,16,768]{2,1,0:T(8,128)} %bitcast.3, f32[16]{0:T(128)} %scale_ref.1), custom_call_target="tpu_custom_call" | custom-call | flops 20000000000 | bytes 4000000 | tf_op jit(solution)/shard_map/pallas_call | solution.py:254
  141.7 1.3 copy.6

commit v3 on v2

v3 whole, which is shorter than its diff:
```python
import functools

import jax
import jax.numpy as jnp
from jax import lax
from jax.experimental import pallas as pl
from jax.experimental.pallas import tpu as pltpu
from jax.sharding import PartitionSpec as P

MESH = pl.DeviceIdType.MESH
FIRST, LAST = 4, 4
XN, CR = 2, 3
L = dict(z_own=3, z_relay=1, x_own=4, x_far=-1, x_relay_own=-1, x_relay_near=-1, x_relay_far=-2, c_own=3, c_pair=1, c_near=1, c_near2=0, c_far=0, c_far2=-2, products_c=-3, products_b=-3)
XT = ((-4, -2, 5, 8, 11, 14, 7, 10, 13, 16, 18), (-4, -2, 9, 10, 11, 12, 11, 12, 13, 14, 16))
B_RELAY, B_NEAR, B_FAR, B_SPREAD, B_LAST, B_KINDS = 0, 1, 2, 3, 7, 8
C_PAIR, C_NEAR, C_FAR, C_CORE, C_KINDS = 0, 1, 3, 5, 6
NT = (((1,), (1,)), ((), ()))


def split(v):
    high = v.astype(jnp.bfloat16)
    return high, (v - high.astype(jnp.float32)).astype(jnp.bfloat16)


def kernel(
    w_ref, c_ref, b_ref, scale_ref, out_ref,
    cbuf, bbuf, wfull, whigh, wlow, thigh, tlow, sig, part1, half, part2, turned,
    load_sem, c_recv, b_recv, c_send, b_send, recv1, recv2, send1, send2,
):
    orbitals, states, aux = c_ref.shape
    row, col = lax.axis_index("row"), lax.axis_index("col")
    x, zh = row // 4, row % 4
    y, zl, core = col // 4, (col // 2) % 2, col % 2

    def row_of(x_at, zh_at):
        return (x_at + 4) % 4 * 4 + (zh_at + 4) % 4

    def col_of(y_at, zl_at, core_at):
        return (y_at + 4) % 4 * 4 + zl_at * 2 + core_at

    barrier = pltpu.get_barrier_semaphore()
    for step in range(1, 16):
        pl.semaphore_signal(barrier, inc=1, device_id=(row, (col + step) % 16), device_id_type=MESH)
        pl.semaphore_signal(barrier, inc=1, device_id=((row + step) % 16, col), device_id_type=MESH)

    loads = [
        pltpu.make_async_copy(w_ref, wfull, load_sem.at[0]),
        pltpu.make_async_copy(c_ref, cbuf.at[col], load_sem.at[1]),
        pltpu.make_async_copy(b_ref, bbuf.at[row], load_sem.at[2]),
    ]
    for load in loads:
        load.start()
    sig[...] = jnp.zeros_like(sig)
    pl.semaphore_wait(barrier, 30)

    def c_copy(g, piece, edge, kind, to, own=False):
        return pltpu.make_async_remote_copy(
            src_ref=c_ref.at[g] if own else cbuf.at[piece, g],
            dst_ref=cbuf.at[piece, g],
            send_sem=c_send.at[edge],
            recv_sem=c_recv.at[kind, g],
            device_id=(row, to),
            device_id_type=MESH,
        )

    def b_copy(g, piece, edge, kind, to, own=False):
        return pltpu.make_async_remote_copy(
            src_ref=b_ref.at[g] if own else bbuf.at[piece, g],
            dst_ref=bbuf.at[piece, g],
            send_sem=b_send.at[edge],
            recv_sem=b_recv.at[kind, g],
            device_id=(to, col),
            device_id_type=MESH,
        )

    def got_c(g, kind, pieces=1):
        block = cbuf.at[pl.ds(0, pieces), g]
        pltpu.make_async_copy(block, block, c_recv.at[kind, g]).wait()

    def got_b(g, kind, pieces=1):
        block = bbuf.at[pl.ds(0, pieces), g]
        pltpu.make_async_copy(block, block, b_recv.at[kind, g]).wait()

    def way_of(g):
        return 1 - 2 * (g % 2)

    def z_own(g):
        way = way_of(g)
        b_copy(g, row, 0, B_RELAY, row_of(x, zh + way), True).start()
        b_copy(g, row, 1, B_NEAR, row_of(x, zh - way), True).start()

    def z_relay(g):
        way = way_of(g)
        got_b(g, B_RELAY)
        b_copy(g, row_of(x, zh - way), 4, B_FAR, row_of(x, zh + way)).start()

    def x_own(g):
        way = way_of(g)
        b_copy(g, row, 2, B_SPREAD, row_of(x + way, zh), True).start()
        b_copy(g, row, 3, B_LAST, row_of(x - way, zh), True).start()

    def x_near(g):
        way = way_of(g)
        got_b(g, B_NEAR)
        for at in range(2):
            piece = row_of(x, zh - way + 2 * at * way)
            b_copy(g, piece, 5 + 2 * at, B_SPREAD + 1, row_of(x + way, zh)).start()
            b_copy(g, piece, 6 + 2 * at, B_LAST, row_of(x - way, zh)).start()

    def x_far(g):
        way = way_of(g)
        got_b(g, B_FAR)
        piece = row_of(x, zh + 2)
        b_copy(g, piece, 10, B_SPREAD + 3, row_of(x + way, zh)).start()
        b_copy(g, piece, 11, B_LAST, row_of(x - way, zh)).start()

    def x_relay_own(g):
        way = way_of(g)
        got_b(g, B_SPREAD)
        b_copy(g, row_of(x - way, zh), 9, B_LAST, row_of(x + way, zh)).start()

    def x_relay_near(g):
        way = way_of(g)
        got_b(g, B_SPREAD + 1, 2)
        for at in range(2):
            piece = row_of(x - way, zh - 1 + 2 * at)
            b_copy(g, piece, 12 + at, B_LAST, row_of(x + way, zh)).start()

    def x_relay_far(g):
        way = way_of(g)
        got_b(g, B_SPREAD + 3)
        b_copy(g, row_of(x - way, zh + 2), 14, B_LAST, row_of(x + way, zh)).start()

    def x_offset(at, way):
        return (0, -way, way, 2)[at]

    def first_x_own(g):
        way = way_of(g)
        b_copy(g, row, 0, B_RELAY, row_of(x + way, zh), True).start()
        b_copy(g, row, 1, B_NEAR, row_of(x - way, zh), True).start()

    def first_x_relay(g):
        way = way_of(g)
        got_b(g, B_RELAY)
        b_copy(g, row_of(x - way, zh), 10, B_FAR, row_of(x + way, zh)).start()

    def then_z(g, at, own):
        way = way_of(g)
        piece = row_of(x + x_offset(at, way), zh)
        b_copy(g, piece, 2 + 2 * at, B_SPREAD + at, row_of(x, zh + way), own).start()
        b_copy(g, piece, 3 + 2 * at, B_LAST, row_of(x, zh - way), own).start()

    def then_z_relay(g, at):
        way = way_of(g)
        got_b(g, B_SPREAD + at)
        piece = row_of(x + x_offset(at, way), zh - way)
        b_copy(g, piece, 11 + at, B_LAST, row_of(x, zh + way)).start()

    def c_own(g):
        c_copy(g, col, 0, C_PAIR, col_of(y, 1 - zl, core), True).start()
        c_copy(g, col, 1, C_NEAR, col_of(y + 1, zl, core), True).start()
        c_copy(g, col, 2, C_NEAR, col_of(y - 1, zl, core), True).start()
        c_copy(g, col, 3, C_CORE, col_of(y, zl, 1 - core), True).start()

    def c_pair(g):
        got_c(g, C_PAIR)
        piece = col_of(y, 1 - zl, core)
        c_copy(g, piece, 4, C_NEAR + 1, col_of(y + 1, zl, core)).start()
        c_copy(g, piece, 5, C_NEAR + 1, col_of(y - 1, zl, core)).start()
        c_copy(g, piece, 6, C_CORE, col_of(y, zl, 1 - core)).start()

    def c_spread(g, far):
        way = way_of(g)
        got_c(g, C_NEAR + far, 2)
        zl_at = zl + far - 2 * zl * far
        piece = col_of(y - way, zl_at, core)
        c_copy(g, piece, 7 + far, C_FAR + far, col_of(y + way, zl, core)).start()
        c_copy(g, piece, 9 + far, C_CORE, col_of(y, zl, 1 - core)).start()
        piece = col_of(y + way, zl_at, core)
        c_copy(g, piece, 11 + far, C_CORE, col_of(y, zl, 1 - core)).start()

    def c_far(g, far):
        got_c(g, C_FAR + far)
        piece = col_of(y + 2, zl + far - 2 * zl * far, core)
        c_copy(g, piece, 13 + far, C_CORE, col_of(y, zl, 1 - core)).start()

    def products_c(g):
        got_c(g, C_CORE, 8)
        c_high, c_low = split(cbuf[:, g].reshape(16 * states, aux))
        t = jnp.dot(c_high, whigh[...], preferred_element_type=jnp.float32)
        t += jnp.dot(c_high, wlow[...], preferred_element_type=jnp.float32)
        t += jnp.dot(c_low, whigh[...], preferred_element_type=jnp.float32)
        t_high, t_low = split(t * scale_ref[g])
        thigh[g] = t_high
        tlow[g] = t_low

    def products_b(g):
        got_b(g, B_LAST, 8)
        b_high, b_low = split(bbuf[:, g].reshape(16 * states, aux))
        s = lax.dot_general(b_high, thigh[g], NT, preferred_element_type=jnp.float32)
        s += lax.dot_general(b_high, tlow[g], NT, preferred_element_type=jnp.float32)
        s += lax.dot_general(b_low, thigh[g], NT, preferred_element_type=jnp.float32)
        sig[...] += s

    @pl.loop(0, orbitals + FIRST + LAST)
    def tick(step):
        t = step - FIRST

        def when(g, first, do):
            @pl.when((g >= first) & (g < orbitals))
            def _():
                do(g)

        def c_when(lead, do):
            at = t + lead
            first = at + at // CR

            @pl.when((at >= 0) & (first < orbitals))
            def _():
                do(first)

            @pl.when((at >= 0) & (at % CR == CR - 1) & (first + 1 < orbitals))
            def _():
                do(first + 1)

        def at_tick(ticks, do, *args):
            @pl.when(t == ticks)
            def _():
                do(*args)

        when(t + L["z_own"], XN, z_own)
        for g in range(XN):
            at_tick(XT[g][0], first_x_own, g)
        when(t + L["x_own"], XN, x_own)
        c_when(L["c_own"], c_own)

        @pl.when(step == 0)
        def _():
            for load in loads:
                load.wait()
            w_high, w_low = split(wfull[...])
            whigh[...] = w_high
            wlow[...] = w_low

        when(t + L["z_relay"], XN, z_relay)
        when(t, XN, x_near)
        when(t + L["x_far"], XN, x_far)
        when(t + L["x_relay_own"], XN, x_relay_own)
        when(t + L["x_relay_near"], XN, x_relay_near)
        when(t + L["x_relay_far"], XN, x_relay_far)
        for g in range(XN):
            at_tick(XT[g][1], first_x_relay, g)
            for at in range(4):
                if at == 1:
                    at_tick(XT[g][2 + at], got_b, g, B_NEAR)
                if at == 3:
                    at_tick(XT[g][2 + at], got_b, g, B_FAR)
                at_tick(XT[g][2 + at], then_z, g, at, at == 0)
                at_tick(XT[g][6 + at], then_z_relay, g, at)
        c_when(L["c_pair"], c_pair)
        c_when(L["c_near"], lambda g: c_spread(g, 0))
        c_when(L["c_near2"], lambda g: c_spread(g, 1))
        c_when(L["c_far"], lambda g: c_far(g, 0))
        c_when(L["c_far2"], lambda g: c_far(g, 1))
        c_when(L["products_c"], products_c)
        when(t + L["products_b"], XN, products_b)
        for g in range(XN):
            at_tick(XT[g][10], products_b, g)

    def copy1(step):
        to = (col + step) % 16
        return pltpu.make_async_remote_copy(
            src_ref=sig.at[pl.ds(pl.multiple_of(to * states, states), states)],
            dst_ref=part1.at[col],
            send_sem=send1,
            recv_sem=recv1,
            device_id=(row, to),
            device_id_type=MESH,
        )

    def copy2(step):
        to = (row + step) % 16
        return pltpu.make_async_remote_copy(
            src_ref=half.at[to // 8],
            dst_ref=part2.at[row],
            send_sem=send2,
            recv_sem=recv2,
            device_id=(to, col),
            device_id_type=MESH,
        )

    def wait_all(parts, semaphore):
        others = parts.at[pl.ds(0, 15)]
        pltpu.make_async_copy(others, others, semaphore).wait()

    for step in range(1, 16):
        copy1(step).start()
    part1[col] = sig[pl.ds(pl.multiple_of(col * states, states), states), :]
    wait_all(part1, recv1)
    total = jnp.sum(part1[...], axis=0)
    half[0] = total[:, :128]
    half[1] = total[:, 128:]
    for step in range(1, 16):
        copy2(step).start()
    part2[row] = half[row // 8]
    wait_all(part2, recv2)
    turned[...] = jnp.sum(part2[...], axis=0).T
    out_ref[...] = turned[pl.ds(pl.multiple_of(row % 8 * states, states), states), :]

    wait_all(part1, send1)
    wait_all(part2, send2)
    for edge in range(15):
        pltpu.make_async_copy(c_ref, cbuf.at[0], c_send.at[edge]).wait()
        pltpu.make_async_copy(b_ref, bbuf.at[0], b_send.at[edge]).wait()


def body(screened, fit_coeffs, coulomb_factors, orbital_weights):
    orbitals, aux, states = fit_coeffs.shape
    f32, bf16 = jnp.float32, jnp.bfloat16
    dma = pltpu.SemaphoreType.DMA
    return pl.pallas_call(
        kernel,
        out_shape=jax.ShapeDtypeStruct((states, states), f32),
        in_specs=[pl.BlockSpec(memory_space=pl.ANY)] * 3 + [pl.BlockSpec(memory_space=pltpu.SMEM)],
        out_specs=pl.BlockSpec(memory_space=pltpu.VMEM),
        scratch_shapes=[
            pltpu.VMEM((16, orbitals, states, aux), f32),
            pltpu.VMEM((16, orbitals, states, aux), f32),
            pltpu.VMEM((aux, aux), f32),
            pltpu.VMEM((aux, aux), bf16),
            pltpu.VMEM((aux, aux), bf16),
            pltpu.VMEM((orbitals, 16 * states, aux), bf16),
            pltpu.VMEM((orbitals, 16 * states, aux), bf16),
            pltpu.VMEM((16 * states, 16 * states), f32),
            pltpu.VMEM((16, states, 16 * states), f32),
            pltpu.VMEM((2, states, 128), f32),
            pltpu.VMEM((16, states, 128), f32),
            pltpu.VMEM((128, states), f32),
            dma((3,)),
            dma((C_KINDS, orbitals)),
            dma((B_KINDS, orbitals)),
            dma((15,)),
            dma((15,)),
            dma,
            dma,
            dma,
            dma,
        ],
        compiler_params=pltpu.CompilerParams(
            collective_id=0, has_side_effects=True, vmem_limit_bytes=63 * 1024 * 1024
        ),
        cost_estimate=pl.CostEstimate(flops=20_000_000_000, bytes_accessed=4_000_000, transcendentals=0),
    )(
        screened,
        jnp.transpose(fit_coeffs, (0, 2, 1)),
        jnp.transpose(coulomb_factors, (0, 2, 1)),
        orbital_weights,
    )


def solution(mesh):
    placed = (P("row", "col"), P(None, "row", "col"), P(None, "col", "row"), P())
    return jax.shard_map(
        body, mesh=mesh, in_specs=placed, out_specs=P("row", "col"), check_vma=False
    )
```

time: 143 us -> 132 us (0.923)
  Pallas kernels: 142 us -> 130 us
    pallas_call x1, Pallas kernels: 142 us -> 130 us  [body(): pl.pallas_call(kernel, out_shape=jax.ShapeDtypeStruct((states, states), f...]
where the time goes in v3:
time: 132 us; the launch traced here: 131 us
  Pallas kernels  130 us (98%)
    pallas_call x1, Pallas kernels, body(): pl.pallas_call(kernel, out_shape=jax.ShapeDtypeStruct((states, states), f...  130 us

profile of v3, /device:TPU:1, one launch (start us, length us, event | category | flops | bytes accessed | tf_op | source)
XLA Modules:
  0.0 131.3 jit_solution(7487981961049069845)
XLA Ops:
  0.0 130.0 %shard_map.46 = f32[16,16]{1,0:T(8,128)} custom-call(f32[768,768]{1,0:T(8,128)} %w_ref.1, f32[16,16,768]{2,1,0:T(8,128)} %bitcast.2, f32[16,16,768]{2,1,0:T(8,128)} %bitcast.3, f32[16]{0:T(128)} %scale_ref.1), custom_call_target="tpu_custom_call" | custom-call | flops 20000000000 | bytes 4000000 | tf_op jit(solution)/shard_map/pallas_call | solution.py:321
  130.0 1.3 copy.6

commit v4 on v3

--- a/solution.py
+++ b/solution.py
@@ -8,10 +8,13 @@
 from jax.sharding import PartitionSpec as P
 
 MESH = pl.DeviceIdType.MESH
-FIRST, LAST = 4, 4
-XN, CR = 2, 3
-L = dict(z_own=3, z_relay=1, x_own=4, x_far=-1, x_relay_own=-1, x_relay_near=-1, x_relay_far=-2, c_own=3, c_pair=1, c_near=1, c_near2=0, c_far=0, c_far2=-2, products_c=-3, products_b=-3)
-XT = ((-4, -2, 5, 8, 11, 14, 7, 10, 13, 16, 18), (-4, -2, 9, 10, 11, 12, 11, 12, 13, 14, 16))
+FIRST, LAST = 1, 6
+XN, CR, W_AT = 2, 2, 1
+L = dict(
+    z_own=3, z_relay=1, x_own=6, x_far=-1, x_relay_own=0, x_relay_near=-1, x_relay_far=-3,
+    c_own=0, c_pair=-1, c_near=-1, c_near2=-2, c_far=-2, c_far2=-4, products_c=-5, products_b=-5,
+)
+XT = ((0, 2, 5, 8, 11, 14, 7, 10, 13, 16, 18), (0, 3, 9, 11, 12, 13, 11, 13, 14, 15, 17))
 B_RELAY, B_NEAR, B_FAR, B_SPREAD, B_LAST, B_KINDS = 0, 1, 2, 3, 7, 8
 C_PAIR, C_NEAR, C_FAR, C_CORE, C_KINDS = 0, 1, 3, 5, 6
 NT = (((1,), (1,)), ((), ()))
@@ -53,21 +56,21 @@
     sig[...] = jnp.zeros_like(sig)
     pl.semaphore_wait(barrier, 30)
 
-    def c_copy(g, piece, edge, kind, to, own=False):
+    def c_copy(g, piece, kind, to, own=False):
         return pltpu.make_async_remote_copy(
             src_ref=c_ref.at[g] if own else cbuf.at[piece, g],
             dst_ref=cbuf.at[piece, g],
-            send_sem=c_send.at[edge],
+            send_sem=c_send,
             recv_sem=c_recv.at[kind, g],
             device_id=(row, to),
             device_id_type=MESH,
         )
 
-    def b_copy(g, piece, edge, kind, to, own=False):
+    def b_copy(g, piece, kind, to, own=False):
         return pltpu.make_async_remote_copy(
             src_ref=b_ref.at[g] if own else bbuf.at[piece, g],
             dst_ref=bbuf.at[piece, g],
-            send_sem=b_send.at[edge],
+            send_sem=b_send,
             recv_sem=b_recv.at[kind, g],
             device_id=(to, col),
             device_id_type=MESH,
@@ -86,103 +89,103 @@
 
     def z_own(g):
         way = way_of(g)
-        b_copy(g, row, 0, B_RELAY, row_of(x, zh + way), True).start()
-        b_copy(g, row, 1, B_NEAR, row_of(x, zh - way), True).start()
+        b_copy(g, row, B_RELAY, row_of(x, zh + way), True).start()
+        b_copy(g, row, B_NEAR, row_of(x, zh - way), True).start()
 
     def z_relay(g):
         way = way_of(g)
         got_b(g, B_RELAY)
-        b_copy(g, row_of(x, zh - way), 4, B_FAR, row_of(x, zh + way)).start()
+        b_copy(g, row_of(x, zh - way), B_FAR, row_of(x, zh + way)).start()
 
     def x_own(g):
         way = way_of(g)
-        b_copy(g, row, 2, B_SPREAD, row_of(x + way, zh), True).start()
-        b_copy(g, row, 3, B_LAST, row_of(x - way, zh), True).start()
+        b_copy(g, row, B_SPREAD, row_of(x + way, zh), True).start()
+        b_copy(g, row, B_LAST, row_of(x - way, zh), True).start()
 
     def x_near(g):
         way = way_of(g)
         got_b(g, B_NEAR)
         for at in range(2):
             piece = row_of(x, zh - way + 2 * at * way)
-            b_copy(g, piece, 5 + 2 * at, B_SPREAD + 1, row_of(x + way, zh)).start()
-            b_copy(g, piece, 6 + 2 * at, B_LAST, row_of(x - way, zh)).start()
+            b_copy(g, piece, B_SPREAD + 1, row_of(x + way, zh)).start()
+            b_copy(g, piece, B_LAST, row_of(x - way, zh)).start()
 
     def x_far(g):
         way = way_of(g)
         got_b(g, B_FAR)
         piece = row_of(x, zh + 2)
-        b_copy(g, piece, 10, B_SPREAD + 3, row_of(x + way, zh)).start()
-        b_copy(g, piece, 11, B_LAST, row_of(x - way, zh)).start()
+        b_copy(g, piece, B_SPREAD + 3, row_of(x + way, zh)).start()
+        b_copy(g, piece, B_LAST, row_of(x - way, zh)).start()
 
     def x_relay_own(g):
         way = way_of(g)
         got_b(g, B_SPREAD)
-        b_copy(g, row_of(x - way, zh), 9, B_LAST, row_of(x + way, zh)).start()
+        b_copy(g, row_of(x - way, zh), B_LAST, row_of(x + way, zh)).start()
 
     def x_relay_near(g):
         way = way_of(g)
         got_b(g, B_SPREAD + 1, 2)
         for at in range(2):
             piece = row_of(x - way, zh - 1 + 2 * at)
-            b_copy(g, piece, 12 + at, B_LAST, row_of(x + way, zh)).start()
+            b_copy(g, piece, B_LAST, row_of(x + way, zh)).start()
 
     def x_relay_far(g):
         way = way_of(g)
         got_b(g, B_SPREAD + 3)
-        b_copy(g, row_of(x - way, zh + 2), 14, B_LAST, row_of(x + way, zh)).start()
+        b_copy(g, row_of(x - way, zh + 2), B_LAST, row_of(x + way, zh)).start()
 
     def x_offset(at, way):
         return (0, -way, way, 2)[at]
 
     def first_x_own(g):
         way = way_of(g)
-        b_copy(g, row, 0, B_RELAY, row_of(x + way, zh), True).start()
-        b_copy(g, row, 1, B_NEAR, row_of(x - way, zh), True).start()
+        b_copy(g, row, B_RELAY, row_of(x + way, zh), True).start()
+        b_copy(g, row, B_NEAR, row_of(x - way, zh), True).start()
 
     def first_x_relay(g):
         way = way_of(g)
         got_b(g, B_RELAY)
-        b_copy(g, row_of(x - way, zh), 10, B_FAR, row_of(x + way, zh)).start()
+        b_copy(g, row_of(x - way, zh), B_FAR, row_of(x + way, zh)).start()
 
     def then_z(g, at, own):
         way = way_of(g)
         piece = row_of(x + x_offset(at, way), zh)
-        b_copy(g, piece, 2 + 2 * at, B_SPREAD + at, row_of(x, zh + way), own).start()
-        b_copy(g, piece, 3 + 2 * at, B_LAST, row_of(x, zh - way), own).start()
+        b_copy(g, piece, B_SPREAD + at, row_of(x, zh + way), own).start()
+        b_copy(g, piece, B_LAST, row_of(x, zh - way), own).start()
 
     def then_z_relay(g, at):
         way = way_of(g)
         got_b(g, B_SPREAD + at)
         piece = row_of(x + x_offset(at, way), zh - way)
-        b_copy(g, piece, 11 + at, B_LAST, row_of(x, zh + way)).start()
+        b_copy(g, piece, B_LAST, row_of(x, zh + way)).start()
 
     def c_own(g):
-        c_copy(g, col, 0, C_PAIR, col_of(y, 1 - zl, core), True).start()
-        c_copy(g, col, 1, C_NEAR, col_of(y + 1, zl, core), True).start()
-        c_copy(g, col, 2, C_NEAR, col_of(y - 1, zl, core), True).start()
-        c_copy(g, col, 3, C_CORE, col_of(y, zl, 1 - core), True).start()
+        c_copy(g, col, C_PAIR, col_of(y, 1 - zl, core), True).start()
+        c_copy(g, col, C_NEAR, col_of(y + 1, zl, core), True).start()
+        c_copy(g, col, C_NEAR, col_of(y - 1, zl, core), True).start()
+        c_copy(g, col, C_CORE, col_of(y, zl, 1 - core), True).start()
 
     def c_pair(g):
         got_c(g, C_PAIR)
         piece = col_of(y, 1 - zl, core)
-        c_copy(g, piece, 4, C_NEAR + 1, col_of(y + 1, zl, core)).start()
-        c_copy(g, piece, 5, C_NEAR + 1, col_of(y - 1, zl, core)).start()
-        c_copy(g, piece, 6, C_CORE, col_of(y, zl, 1 - core)).start()
+        c_copy(g, piece, C_NEAR + 1, col_of(y + 1, zl, core)).start()
+        c_copy(g, piece, C_NEAR + 1, col_of(y - 1, zl, core)).start()
+        c_copy(g, piece, C_CORE, col_of(y, zl, 1 - core)).start()
 
     def c_spread(g, far):
         way = way_of(g)
         got_c(g, C_NEAR + far, 2)
         zl_at = zl + far - 2 * zl * far
         piece = col_of(y - way, zl_at, core)
-        c_copy(g, piece, 7 + far, C_FAR + far, col_of(y + way, zl, core)).start()
-        c_copy(g, piece, 9 + far, C_CORE, col_of(y, zl, 1 - core)).start()
+        c_copy(g, piece, C_FAR + far, col_of(y + way, zl, core)).start()
+        c_copy(g, piece, C_CORE, col_of(y, zl, 1 - core)).start()
         piece = col_of(y + way, zl_at, core)
-        c_copy(g, piece, 11 + far, C_CORE, col_of(y, zl, 1 - core)).start()
+        c_copy(g, piece, C_CORE, col_of(y, zl, 1 - core)).start()
 
     def c_far(g, far):
         got_c(g, C_FAR + far)
         piece = col_of(y + 2, zl + far - 2 * zl * far, core)
-        c_copy(g, piece, 13 + far, C_CORE, col_of(y, zl, 1 - core)).start()
+        c_copy(g, piece, C_CORE, col_of(y, zl, 1 - core)).start()
 
     def products_c(g):
         got_c(g, C_CORE, 8)
@@ -202,10 +205,18 @@
         s += lax.dot_general(b_low, thigh[g], NT, preferred_element_type=jnp.float32)
         sig[...] += s
 
-    @pl.loop(0, orbitals + FIRST + LAST)
-    def tick(step):
-        t = step - FIRST
-
+    z_own(XN)
+    for g in range(XN):
+        first_x_own(g)
+    for g in range(XN + 1, FIRST + L["z_own"]):
+        z_own(g)
+    for g in range(XN, FIRST + L["x_own"]):
+        x_own(g)
+    for at in range(FIRST + L["c_own"]):
+        c_own(at + at // CR)
+
+    @pl.loop(FIRST, orbitals + LAST)
+    def tick(t):
         def when(g, first, do):
             @pl.when((g >= first) & (g < orbitals))
             def _():
@@ -229,18 +240,8 @@
                 do(*args)
 
         when(t + L["z_own"], XN, z_own)
-        for g in range(XN):
-            at_tick(XT[g][0], first_x_own, g)
         when(t + L["x_own"], XN, x_own)
         c_when(L["c_own"], c_own)
-
-        @pl.when(step == 0)
-        def _():
-            for load in loads:
-                load.wait()
-            w_high, w_low = split(wfull[...])
-            whigh[...] = w_high
-            wlow[...] = w_low
 
         when(t + L["z_relay"], XN, z_relay)
         when(t, XN, x_near)
@@ -257,6 +258,14 @@
                     at_tick(XT[g][2 + at], got_b, g, B_FAR)
                 at_tick(XT[g][2 + at], then_z, g, at, at == 0)
                 at_tick(XT[g][6 + at], then_z_relay, g, at)
+        @pl.when(t == W_AT)
+        def _():
+            for load in loads:
+                load.wait()
+            w_high, w_low = split(wfull[...])
+            whigh[...] = w_high
+            wlow[...] = w_low
+
         c_when(L["c_pair"], c_pair)
         c_when(L["c_near"], lambda g: c_spread(g, 0))
         c_when(L["c_near2"], lambda g: c_spread(g, 1))
@@ -309,9 +318,8 @@
 
     wait_all(part1, send1)
     wait_all(part2, send2)
-    for edge in range(15):
-        pltpu.make_async_copy(c_ref, cbuf.at[0], c_send.at[edge]).wait()
-        pltpu.make_async_copy(b_ref, bbuf.at[0], b_send.at[edge]).wait()
+    wait_all(cbuf, c_send)
+    wait_all(bbuf, b_send)
 
 
 def body(screened, fit_coeffs, coulomb_factors, orbital_weights):
@@ -339,8 +347,8 @@
             dma((3,)),
             dma((C_KINDS, orbitals)),
             dma((B_KINDS, orbitals)),
-            dma((15,)),
-            dma((15,)),
+            dma,
+            dma,
             dma,
             dma,
             dma,

time: 132 us -> 126 us (0.955)
  Pallas kernels: 130 us -> 124 us
    pallas_call x1, Pallas kernels: 130 us -> 124 us  [body(): pl.pallas_call(kernel, out_shape=jax.ShapeDtypeStruct((states, states), f...]
where the time goes in v4:
time: 126 us
  Pallas kernels  124 us (98%)
  local copies, waits for them, and re-layouts  1.3 us (1%)
    pallas_call x1, Pallas kernels, body(): pl.pallas_call(kernel, out_shape=jax.ShapeDtypeStruct((states, states), f...  124 us

profile of v4, /device:TPU:1, one launch (start us, length us, event | category | flops | bytes accessed | tf_op | source)
XLA Modules:
  0.0 125.7 jit_solution(3894650338306612125)
XLA Ops:
  0.0 124.4 %shard_map.46 = f32[16,16]{1,0:T(8,128)} custom-call(f32[768,768]{1,0:T(8,128)} %w_ref.1, f32[16,16,768]{2,1,0:T(8,128)} %bitcast.2, f32[16,16,768]{2,1,0:T(8,128)} %bitcast.3, f32[16]{0:T(128)} %scale_ref.1), custom_call_target="tpu_custom_call" | custom-call | flops 20000000000 | bytes 4000000 | tf_op jit(solution)/shard_map/pallas_call | solution.py:329
  124.4 1.3 %copy.6 = f32[16,16]{1,0:T(8,128)} copy(f32[16,16]{1,0:T(8,128)} %shard_map.46) | data formatting | bytes 2048

commit v5 on v4

--- a/solution.py
+++ b/solution.py
@@ -8,11 +8,11 @@
 from jax.sharding import PartitionSpec as P
 
 MESH = pl.DeviceIdType.MESH
-FIRST, LAST = 1, 6
+FIRST, LAST = 1, 5
 XN, CR, W_AT = 2, 2, 1
 L = dict(
-    z_own=3, z_relay=1, x_own=6, x_far=-1, x_relay_own=0, x_relay_near=-1, x_relay_far=-3,
-    c_own=0, c_pair=-1, c_near=-1, c_near2=-2, c_far=-2, c_far2=-4, products_c=-5, products_b=-5,
+    z_own=3, z_relay=1, x_own=6, x_far=-1, x_relay_own=0, x_relay_near=-1, x_relay_far=-2,
+    c_own=0, c_pair=-1, c_near=-1, c_near2=-2, c_far=-2, c_far2=-3, products_c=-5, products_b=-4,
 )
 XT = ((0, 2, 5, 8, 11, 14, 7, 10, 13, 16, 18), (0, 3, 9, 11, 12, 13, 11, 13, 14, 15, 17))
 B_RELAY, B_NEAR, B_FAR, B_SPREAD, B_LAST, B_KINDS = 0, 1, 2, 3, 7, 8

time: 126 us -> 125 us (level)
  no operation moved by 1% of the time
where the time goes in v5:
time: 125 us
  Pallas kernels  124 us (99%)
  local copies, waits for them, and re-layouts  1.3 us (1%)
    pallas_call x1, Pallas kernels, body(): pl.pallas_call(kernel, out_shape=jax.ShapeDtypeStruct((states, states), f...  124 us

profile of v5, /device:TPU:1, one launch (start us, length us, event | category | flops | bytes accessed | tf_op | source)
XLA Modules:
  0.0 125.1 jit_solution(14716047754705252332)
XLA Ops:
  0.0 123.8 %shard_map.46 = f32[16,16]{1,0:T(8,128)} custom-call(f32[768,768]{1,0:T(8,128)} %w_ref.1, f32[16,16,768]{2,1,0:T(8,128)} %bitcast.2, f32[16,16,768]{2,1,0:T(8,128)} %bitcast.3, f32[16]{0:T(128)} %scale_ref.1), custom_call_target="tpu_custom_call" | custom-call | flops 20000000000 | bytes 4000000 | tf_op jit(solution)/shard_map/pallas_call | solution.py:329
  123.8 1.3 %copy.6 = f32[16,16]{1,0:T(8,128)} copy(f32[16,16]{1,0:T(8,128)} %shard_map.46) | data formatting | bytes 2048

commit v6 on v5

--- a/solution.py
+++ b/solution.py
@@ -190,9 +190,10 @@
     def products_c(g):
         got_c(g, C_CORE, 8)
         c_high, c_low = split(cbuf[:, g].reshape(16 * states, aux))
-        t = jnp.dot(c_high, whigh[...], preferred_element_type=jnp.float32)
-        t += jnp.dot(c_high, wlow[...], preferred_element_type=jnp.float32)
-        t += jnp.dot(c_low, whigh[...], preferred_element_type=jnp.float32)
+        c_both = jnp.concatenate([c_high, c_low], axis=0)
+        both = jnp.dot(c_both, whigh[...], preferred_element_type=jnp.float32)
+        t = jnp.dot(c_high, wlow[...], preferred_element_type=jnp.float32)
+        t += both[: 16 * states] + both[16 * states :]
         t_high, t_low = split(t * scale_ref[g])
         thigh[g] = t_high
         tlow[g] = t_low
@@ -200,9 +201,10 @@
     def products_b(g):
         got_b(g, B_LAST, 8)
         b_high, b_low = split(bbuf[:, g].reshape(16 * states, aux))
-        s = lax.dot_general(b_high, thigh[g], NT, preferred_element_type=jnp.float32)
-        s += lax.dot_general(b_high, tlow[g], NT, preferred_element_type=jnp.float32)
-        s += lax.dot_general(b_low, thigh[g], NT, preferred_element_type=jnp.float32)
+        b_both = jnp.concatenate([b_high, b_low], axis=0)
+        both = lax.dot_general(b_both, thigh[g], NT, preferred_element_type=jnp.float32)
+        s = lax.dot_general(b_high, tlow[g], NT, preferred_element_type=jnp.float32)
+        s += both[: 16 * states] + both[16 * states :]
         sig[...] += s
 
     z_own(XN)

time: 125 us -> 125 us (level)
  no operation moved by 1% of the time
where the time goes in v6:
time: 125 us
  Pallas kernels  124 us (99%)
  local copies, waits for them, and re-layouts  1.3 us (1%)
    pallas_call x1, Pallas kernels, body(): pl.pallas_call(kernel, out_shape=jax.ShapeDtypeStruct((states, states), f...  124 us

profile of v6, /device:TPU:1, one launch (start us, length us, event | category | flops | bytes accessed | tf_op | source)
XLA Modules:
  0.0 125.2 jit_solution(10147168971613145395)
XLA Ops:
  0.0 123.9 %shard_map.46 = f32[16,16]{1,0:T(8,128)} custom-call(f32[768,768]{1,0:T(8,128)} %w_ref.1, f32[16,16,768]{2,1,0:T(8,128)} %bitcast.2, f32[16,16,768]{2,1,0:T(8,128)} %bitcast.3, f32[16]{0:T(128)} %scale_ref.1), custom_call_target="tpu_custom_call" | custom-call | flops 20000000000 | bytes 4000000 | tf_op jit(solution)/shard_map/pallas_call | solution.py:331
  123.9 1.3 %copy.6 = f32[16,16]{1,0:T(8,128)} copy(f32[16,16]{1,0:T(8,128)} %shard_map.46) | data formatting | bytes 2048
